TPU v7x, 256 devices: a whole 4x4x8 slice. The times are simulated.
256 devices in a mesh: frame: 16 (over z_hi, x, core), within: 16 (over y, z_lo).
Axes of the slice: x: 4, y: 4, z: 8 (z_hi: 2, z_lo: 4; z = z_hi * 4 + z_lo), core: 2. Of those that a mesh axis runs over, the one named last changes fastest.
Arguments:
- queries: bfloat16 [16, 1152, 1024], P('frame', 'within'), may hold values from -6 to 6
- keys_in: bfloat16 [16, 1152, 1024], P('frame', 'within'), may hold values from -6 to 6
- values_in: bfloat16 [16, 1152, 1024], P('frame', 'within'), may hold values from -6 to 6
- grad_out: bfloat16 [16, 1152, 1024], P('frame', 'within'), may hold values from -6 to 6
- partners: int32 [16, 2], replicated, may hold values from 0 to 15
- registers: int32 [16], replicated, may hold values from 1 to 288
Outputs:
- grad_queries: bfloat16 [16, 1152, 1024], P('frame', 'within')
- grad_keys: bfloat16 [16, 1152, 1024], P('frame', 'within')
- grad_values: bfloat16 [16, 1152, 1024], P('frame', 'within')
Inputs may be any that keep to these rules, and one draw needn't show every extreme that they name: `partners`: A row may list a group more than once, and may list its own group.
All inputs are finite; a program needn't handle non-finite values.
Results may differ from a plain program's by a relative error of at most 0.012.
Values may be sent and summed in bfloat16 or wider, within the bound.
No kernel may reach another device: no remote copies, remote signals or barrier semaphores. Data moves between devices by JAX's collectives and lax.ppermute only.
A program may use at most 128 MiB of HBM per device.

v0:
```python
import jax
import jax.numpy as jnp
from jax import lax
from jax.sharding import PartitionSpec as P

DH = 64


def local(queries, keys_in, values_in, grad_out, partners, registers):
    q_wide, k_wide, v_wide, d_wide = (
        lax.all_to_all(queries, "within", split_axis=2, concat_axis=1, tiled=True),
        lax.all_to_all(keys_in, "within", split_axis=2, concat_axis=1, tiled=True),
        lax.all_to_all(values_in, "within", split_axis=2, concat_axis=1, tiled=True),
        lax.all_to_all(grad_out, "within", split_axis=2, concat_axis=1, tiled=True),
    )
    seq = q_wide.shape[1]
    cols = q_wide.shape[2]
    heads_here = cols // DH
    scale = DH ** (-0.5)

    def split_heads(block):
        return block.reshape(seq, heads_here, DH)

    query3 = split_heads(q_wide[0])
    key3 = split_heads(k_wide[0])
    value3 = split_heads(v_wide[0])
    cotan3 = split_heads(d_wide[0])
    group = lax.axis_index("frame")
    listed = partners[group]
    positions = jnp.arange(seq, dtype=jnp.int32)
    everyone = jnp.ones((seq,), jnp.float32)
    groups = lax.axis_size("frame") * queries.shape[0]

    def patches(other):
        return (positions >= registers[other]).astype(jnp.float32)

    def logits(keys_here, visible):
        raw = (
            jnp.einsum("qhd,khd->hqk", query3, keys_here, preferred_element_type=jnp.float32)
            * scale
        )
        return jnp.where(visible[None, None, :] > 0, raw, -1e30)

    def stats(state, keys_here, values_here, visible, weight):
        old_top, old_total, old_dsum = state
        raw = logits(keys_here, visible)
        top = jnp.max(raw, axis=2)
        expo = jnp.exp(raw - top[:, :, None])
        dprod = jnp.einsum("qhd,khd->hqk", cotan3, values_here, preferred_element_type=jnp.float32)
        total = weight * jnp.sum(expo, axis=2)
        dsum = weight * jnp.sum(expo * dprod, axis=2)
        new_top = jnp.maximum(old_top, top)
        keep_old = jnp.exp(old_top - new_top)
        keep_new = jnp.exp(top - new_top)
        return (
            new_top,
            old_total * keep_old + total * keep_new,
            old_dsum * keep_old + dsum * keep_new,
        )

    def grads(final, keys_here, values_here, visible, weight):
        top, total, delta = final
        raw = logits(keys_here, visible)
        prob = jnp.exp(raw - top[:, :, None]) / total[:, :, None]
        dprod = jnp.einsum("qhd,khd->hqk", cotan3, values_here, preferred_element_type=jnp.float32)
        dscore = prob * (dprod - delta[:, :, None])
        dscore_low = dscore.astype(jnp.bfloat16)
        dq_add = jnp.einsum(
            "hqk,khd->qhd", dscore_low, keys_here, preferred_element_type=jnp.float32
        ) * (scale * weight)
        prob_low = prob.astype(jnp.bfloat16)
        dk_add = jnp.einsum(
            "hqk,qhd->khd", dscore_low, query3, preferred_element_type=jnp.float32
        ) * (scale * weight)
        dv_add = (
            jnp.einsum("hqk,qhd->khd", prob_low, cotan3, preferred_element_type=jnp.float32)
            * weight
        )
        return (dq_add.reshape(seq, cols), dk_add.reshape(seq, cols), dv_add.reshape(seq, cols))

    blank = jnp.zeros((heads_here, seq), jnp.float32)
    state = stats((blank - 1e30, blank, blank), key3, value3, everyone, 1.0)
    keys_all, values_all = (
        lax.all_gather(k_wide, "frame", axis=0, tiled=True),
        lax.all_gather(v_wide, "frame", axis=0, tiled=True),
    )
    for slot in range(listed.shape[0]):
        other = listed[slot]
        state = stats(
            state, split_heads(keys_all[other]), split_heads(values_all[other]), patches(other), 1.0
        )
    top, total, dsum = state
    final = (top, total, dsum / total)
    own_terms = grads(final, key3, value3, everyone, 1.0)
    empty = jnp.zeros((groups, seq, cols), jnp.float32)
    results = (own_terms[0], empty.at[group].add(own_terms[1]), empty.at[group].add(own_terms[2]))
    for slot in range(listed.shape[0]):
        other = listed[slot]
        added = grads(
            final, split_heads(keys_all[other]), split_heads(values_all[other]), patches(other), 1.0
        )
        results = (
            results[0] + added[0],
            results[1].at[other].add(added[1]),
            results[2].at[other].add(added[2]),
        )
    dq_sum = results[0]
    dk_mine, dv_mine = (
        lax.psum_scatter(results[1], "frame", scatter_dimension=0, tiled=True),
        lax.psum_scatter(results[2], "frame", scatter_dimension=0, tiled=True),
    )
    dq_low = dq_sum.astype(jnp.bfloat16)[None]
    dk_low = dk_mine.astype(jnp.bfloat16)
    dv_low = dv_mine.astype(jnp.bfloat16)
    return (
        lax.all_to_all(dq_low, "within", split_axis=1, concat_axis=2, tiled=True),
        lax.all_to_all(dk_low, "within", split_axis=1, concat_axis=2, tiled=True),
        lax.all_to_all(dv_low, "within", split_axis=1, concat_axis=2, tiled=True),
    )


def solution(mesh):
    placed = (
        P("frame", "within", None),
        P("frame", "within", None),
        P("frame", "within", None),
        P("frame", "within", None),
        P(),
        P(),
    )
    return jax.shard_map(
        local,
        mesh=mesh,
        in_specs=placed,
        out_specs=(
            P("frame", "within", None),
            P("frame", "within", None),
            P("frame", "within", None),
        ),
        check_vma=False,
    )
```

profile of v0, /device:TPU:2, one launch (start us, length us, event | category | flops | bytes accessed | tf_op | source)
XLA Modules:
  0.0 439.2 jit_solution(8207483100817958708)
XLA Ops:
  7.2 1.3 copy.62
  9.0 2.3 reduce.55
  11.8 17.1 %all_to_all.120 = bf16[16,2,2304]{2,1,0:T(2,128)(2,1)S(1)} all-to-all(bf16[16,2,2304]{2,1,0:T(2,128)(2,1)S(1)} %reshape.625), channel_id=1, replica_groups=mesh['frame'=16,'within'=16] {'within'}, dimensions={0} | all-to-all | bytes 294912 | tf_op jit(solution)/shard_map/all_to_all | solution.py:12
  30.8 0.9 all_to_all.93
  31.8 1.2 copy.71
  33.1 2.3 reduce.57
  35.9 11.4 %all_to_all.121 = bf16[16,2,2304]{2,1,0:T(2,128)(2,1)S(1)} all-to-all(bf16[16,2,2304]{2,1,0:T(2,128)(2,1)S(1)} %reshape.621), channel_id=1, replica_groups=mesh['frame'=16,'within'=16] {'within'}, dimensions={0} | all-to-all | bytes 294912 | tf_op jit(solution)/shard_map/all_to_all | solution.py:13
  47.3 0.9 reshape.622
  49.2 0.9 all_to_all.100
  50.6 2.3 reduce.54
  52.9 1.2 reshape.623
  54.1 14.1 %all-to-all-start = ((bf16[16,2,2304]{2,1,0:T(2,128)(2,1)}), bf16[16,2,2304]{2,1,0:T(2,128)(2,1)S(1)}, u32[]{:S(2)}, u32[]{:S(2)}) async-start(bf16[16,2,2304]{2,1,0:T(2,128)(2,1)} %reshape.623), calls=%async_computation | async-start | bytes 294912 | tf_op jit(solution)/shard_map/all_to_all | solution.py:11
  71.4 2.3 reduce.56
  73.7 1.2 reshape.619
  76.6 9.3 %all-to-all-done = bf16[16,2,2304]{2,1,0:T(2,128)(2,1)S(1)} async-done(((bf16[16,2,2304]{2,1,0:T(2,128)(2,1)}), bf16[16,2,2304]{2,1,0:T(2,128)(2,1)S(1)}, u32[]{:S(2)}, u32[]{:S(2)}) %all-to-all-start) | async-done | bytes 147488 | tf_op jit(solution)/shard_map/all_to_all | solution.py:11
  86.0 3.5 all-to-all-start.2
  92.1 0.9 reshape.624
  94.3 3.6 all-to-all-done.2
  100.0 0.9 fusion.89
  101.0 2.4 copy-done.2
  103.4 3.6 fusion.2
  106.9 4.2 fusion.88
  111.2 4.2 fusion.87
  115.4 45.3 %all-gather.5.cloned.1.call-done = bf16[16,1152,64]{1,2,0:T(8,128)(2,1)} async-done(((bf16[1,1152,64]{1,2,0:T(8,128)(2,1)}), bf16[16,1152,64]{1,2,0:T(8,128)(2,1)}) %all-gather.5.cloned.1.call-update) | async-done | bytes 2359312 | tf_op jit(solution)/shard_map/all_gather | solution.py:85
  160.6 6.9 %fusion.3 = (f32[1152]{0:T(1024)S(1)}, f32[1152]{0:T(1024)S(1)}, f32[1152,1152]{0,1:T(8,128)}) fusion(f32[1152,1152]{0,1:T(8,128)} %get-tuple-element.98, f32[1152]{0:T(1024)S(1)} %get-tuple-element.97, bf16[1152,64]{0,1:T(8,128)(2,1)S(1)} %reshape.607, bf16[16,1152,64]{1,2,0:T(8,128)(2,1)} %all-gather.5.cloned.1.call-done, s32[]{:T(128)} %select_n.48), kind=kOutput, calls=%fused_computation.18 | convolution fusion | flops 175175424 | bytes 10926080 | tf_op jit(solution)/shard_map/qhd,khd->hqk/dot_general | solution.py:49
  167.5 5.6 %fusion.4 = (f32[1152]{0:T(1024)S(1)}, f32[1152]{0:T(1024)S(1)}, f32[1152,1152]{0,1:T(8,128)}) fusion(f32[1152,1152]{0,1:T(8,128)S(1)} %copy-done.3, f32[1152]{0:T(1024)S(1)} %get-tuple-element.94, bf16[1152,64]{0,1:T(8,128)(2,1)S(1)} %reshape.607, bf16[16,1152,64]{1,2,0:T(8,128)(2,1)} %all-gather.5.cloned.1.call-done, s32[]{:T(128)} %select_n.50), kind=kOutput, calls=%fused_computation.19 | convolution fusion | flops 175175424 | bytes 10926080 | tf_op jit(solution)/shard_map/qhd,khd->hqk/dot_general | solution.py:49
  173.2 8.1 %multiply_convert_fusion.1 = (bf16[1152,1152]{0,1:T(8,128)(2,1)S(1)}, bf16[1152,1152]{0,1:T(8,128)(2,1)S(1)}, bf16[1152,1152]{0,1:T(8,128)(2,1)S(1)}) fusion(f32[1152,1152]{0,1:T(8,128)} %get-tuple-element.101, f32[1152]{0:T(1024)S(1)} %get-tuple-element.84, f32[1152]{0:T(1024)S(1)} %get-tuple-element.83, f32[1152,1152]{0,1:T(8,128)S(1)} %bitcast.198, ...), kind=kLoop, calls=%fused_computation.6 | loop fusion | flops 19906560 | bytes 39826944 | tf_op jit(solution)/shard_map/convert_element_type | solution.py:67
  181.3 3.0 broadcast_in_dim.64.clone
  184.3 2.3 fusion.48
  186.7 2.8 fusion.53
  189.5 2.9 fusion.57
  192.5 2.9 broadcast_in_dim.64.clone.1
  195.4 6.3 %fusion.20 = f32[16,1152,64]{1,2,0:T(8,128)} fusion(f32[16,1152,64]{1,2,0:T(8,128)} %broadcast_in_dim.64.clone.1, s32[]{:T(128)} %select_n.47, bf16[1152,64]{0,1:T(8,128)(2,1)S(1)} %reshape.607, f32[1152,1152]{0,1:T(8,128)} %copy-done.2, f32[1152]{0:T(1024)S(1)} %get-tuple-element.83, f32[1152]{0:T(1024)S(1)} %get-tuple-element.88, pred[]{:T(512)} %get-tuple-element.91), kind=kOutput, calls=%fused_computation.37 | convolution fusion | flops 173924352 | bytes 5761024 | tf_op jit(solution)/shard_map/hqk,qhd->khd/dot_general | solution.py:76
  201.7 3.5 fusion.32
  205.3 3.6 fusion.44
  208.9 3.1 convolution_multiply_fusion.7
  212.6 1.9 fusion.59
  215.2 6.7 %reduce.58 = bf16[1152,64]{1,0:T(8,128)(2,1)S(1)} reduce(bf16[1152,1,64]{2,1,0:T(2,128)(2,1)S(1)} %bitcast.202, bf16[]{:T(256)} %broadcast.338), dimensions={1}, to_apply=%bitcast.158.reduce_sub_computation | reduce | bytes 294914
  222.7 4.8 %all-to-all-start.4 = ((bf16[16,2,2304]{2,1,0:T(2,128)(2,1)}), bf16[16,2,2304]{2,1,0:T(2,128)(2,1)S(1)}, u32[]{:S(2)}, u32[]{:S(2)}) async-start(bf16[16,2,2304]{2,1,0:T(2,128)(2,1)} %reshape.627), calls=%async_computation.4 | async-start | bytes 294912 | tf_op jit(solution)/shard_map/all_to_all | solution.py:116
  227.5 70.9 %reduce-scatter.3.cloned.1.call-done = f32[1,1152,64]{1,2,0:T(8,128)} async-done(((f32[16,1152,64]{1,2,0:T(8,128)}), f32[1,1152,64]{1,2,0:T(8,128)}) %reduce-scatter.3.cloned.1.call-update) | async-done | bytes 294928 | tf_op jit(solution)/shard_map/reduce_scatter | solution.py:109
  298.4 1.0 convert_element_type.67
  300.1 6.7 %reduce.59 = bf16[1152,64]{1,0:T(8,128)(2,1)S(1)} reduce(bf16[1152,1,64]{2,1,0:T(2,128)(2,1)S(1)} %bitcast.203, bf16[]{:T(256)} %broadcast.338), dimensions={1}, to_apply=%bitcast.160.reduce_sub_computation | reduce | bytes 294914
  307.7 4.5 %all-to-all-start.5 = ((bf16[16,2,2304]{2,1,0:T(2,128)(2,1)}), bf16[16,2,2304]{2,1,0:T(2,128)(2,1)S(1)}, u32[]{:S(2)}, u32[]{:S(2)}) async-start(bf16[16,2,2304]{2,1,0:T(2,128)(2,1)} %reshape.629), calls=%async_computation.6 | async-start | bytes 294912 | tf_op jit(solution)/shard_map/all_to_all | solution.py:117
  312.2 95.0 %reduce-scatter.5.cloned.1.call-done = f32[1,1152,64]{1,2,0:T(8,128)} async-done(((f32[16,1152,64]{1,2,0:T(8,128)}), f32[1,1152,64]{1,2,0:T(8,128)}) %reduce-scatter.5.cloned.1.call-update) | async-done | bytes 294928 | tf_op jit(solution)/shard_map/reduce_scatter | solution.py:110
  407.2 1.0 convert_element_type.71
  408.9 6.7 %reduce.60 = bf16[1152,64]{1,0:T(8,128)(2,1)S(1)} reduce(bf16[1152,1,64]{2,1,0:T(2,128)(2,1)S(1)} %bitcast.201, bf16[]{:T(256)} %broadcast.338), dimensions={1}, to_apply=%bitcast.162.reduce_sub_computation | reduce | bytes 294914
  416.5 4.6 %all-to-all-start.6 = ((bf16[16,2,2304]{2,1,0:T(2,128)(2,1)}), bf16[16,2,2304]{2,1,0:T(2,128)(2,1)S(1)}, u32[]{:S(2)}, u32[]{:S(2)}) async-start(bf16[16,2,2304]{2,1,0:T(2,128)(2,1)} %reshape.631), calls=%async_computation.8 | async-start | bytes 294912 | tf_op jit(solution)/shard_map/all_to_all | solution.py:118
  426.4 3.1 all-to-all-done.6
  (104 shorter events, 25.8 us)
Async XLA Ops:
  7.2 61.0 %copy-start = (s32[16,2]{0,1:T(2,128)S(1)}, s32[16,2]{0,1:T(2,128)}, u32[]{:S(2)}) copy-start(s32[16,2]{0,1:T(2,128)} %param.22) | copy-start | bytes 388
  7.2 43.0 %copy-start.7 = (bf16[1,72,1024]{2,1,0:T(8,128)(2,1)S(1)}, bf16[1,72,1024]{2,1,0:T(8,128)(2,1)}, u32[]{:S(2)}) copy-start(bf16[1,72,1024]{2,1,0:T(8,128)(2,1)} %param.18) | copy-start | bytes 442372
  7.2 99.7 %all-gather.3.cloned.1.call-start = ((), (), s32[]{:S(2)}) async-start(), calls=%async_computation.9 | async-start | bytes 2506752 | tf_op jit(solution)/shard_map/all_gather | solution.py:84
  11.8 59.2 %copy-start.8 = (bf16[1,72,1024]{2,1,0:T(8,128)(2,1)S(1)}, bf16[1,72,1024]{2,1,0:T(8,128)(2,1)}, u32[]{:S(2)}) copy-start(bf16[1,72,1024]{2,1,0:T(8,128)(2,1)} %param.21) | copy-start | bytes 442372
  30.2 45.8 %copy-start.9 = (s32[16]{0:T(128)S(1)}, s32[16]{0:T(128)}, u32[]{:S(2)}) copy-start(s32[16]{0:T(128)} %param.23) | copy-start | bytes 196
  30.4 60.3 %copy-start.10 = (s32[3]{0:T(128)S(1)}, s32[3]{0:T(128)}, u32[]{:S(2)}) copy-start(s32[3]{0:T(128)} %constant.142.clone.1) | copy-start | bytes 40
  31.8 128.8 %all-gather.5.cloned.1.call-start = ((), (), s32[]{:S(2)}) async-start(), calls=%async_computation.10 | async-start | bytes 2506752 | tf_op jit(solution)/shard_map/all_gather | solution.py:85
  54.1 31.9 %all-to-all-start = ((bf16[16,2,2304]{2,1,0:T(2,128)(2,1)}), bf16[16,2,2304]{2,1,0:T(2,128)(2,1)S(1)}, u32[]{:S(2)}, u32[]{:S(2)}) async-start(bf16[16,2,2304]{2,1,0:T(2,128)(2,1)} %reshape.623), calls=%async_computation | async-start | bytes 294912 | tf_op jit(solution)/shard_map/all_to_all | solution.py:11
  86.0 11.9 %all-to-all-start.2 = ((bf16[16,2,2304]{2,1,0:T(2,128)(2,1)}), bf16[16,2,2304]{2,1,0:T(2,128)(2,1)S(1)}, u32[]{:S(2)}, u32[]{:S(2)}) async-start(bf16[16,2,2304]{2,1,0:T(2,128)(2,1)} %reshape.619), calls=%async_computation.2 | async-start | bytes 294912 | tf_op jit(solution)/shard_map/all_to_all | solution.py:14
  89.5 208.9 %reduce-scatter.3.cloned.1.call-start = ((), (), s32[]{:S(2)}) async-start(), calls=%async_computation.11 | async-start | bytes 5013504 | tf_op jit(solution)/shard_map/reduce_scatter | solution.py:109
  101.0 2.4 copy-start.2
  160.6 6.9 %copy-start.3 = (f32[1152,1152]{0,1:T(8,128)S(1)}, f32[1152,1152]{0,1:T(8,128)}, u32[]{:S(2)}) copy-start(f32[1152,1152]{0,1:T(8,128)} %get-tuple-element.95) | copy-start | bytes 15925252
  160.6 12.6 %slice-start = ((s8[5308416]{0:T(1024)(128)(4,1)}), s8[4194304]{0:T(1024)(128)(4,1)S(1)}, s32[]{:S(2)}) async-start(s8[5308416]{0:T(1024)(128)(4,1)} %bitcast.193), calls=%async_computation.13 | async-start | bytes 8388608
  160.6 12.6 %slice-start.4 = ((s8[5308416]{0:T(1024)(128)(4,1)}), s8[4194304]{0:T(1024)(128)(4,1)S(1)}, s32[]{:S(2)}) async-start(s8[5308416]{0:T(1024)(128)(4,1)} %bitcast.197), calls=%async_computation.17 | async-start | bytes 8388608
  167.5 5.7 %slice-start.1 = ((s8[5308416]{0:T(1024)(128)(4,1)}), s8[1114112]{0:T(1024)(128)(4,1)S(1)}, s32[]{:S(2)}) async-start(s8[5308416]{0:T(1024)(128)(4,1)} %bitcast.193), calls=%async_computation.14 | async-start | bytes 2228224
  167.5 5.7 %slice-start.5 = ((s8[5308416]{0:T(1024)(128)(4,1)}), s8[1114112]{0:T(1024)(128)(4,1)S(1)}, s32[]{:S(2)}) async-start(s8[5308416]{0:T(1024)(128)(4,1)} %bitcast.197), calls=%async_computation.18 | async-start | bytes 2228224
  181.3 8.2 %copy-start.5 = (bf16[1152,1152]{0,1:T(8,128)(2,1)}, bf16[1152,1152]{0,1:T(8,128)(2,1)S(1)}, u32[]{:S(2)}) copy-start(bf16[1152,1152]{0,1:T(8,128)(2,1)S(1)} %get-tuple-element.85) | copy-start | bytes 7962628
  181.3 8.2 %copy-start.4 = (bf16[1152,1152]{0,1:T(8,128)(2,1)}, bf16[1152,1152]{0,1:T(8,128)(2,1)S(1)}, u32[]{:S(2)}) copy-start(bf16[1152,1152]{0,1:T(8,128)(2,1)S(1)} %get-tuple-element.86) | copy-start | bytes 7962628
  192.4 214.8 %reduce-scatter.5.cloned.1.call-start = ((), (), s32[]{:S(2)}) async-start(), calls=%async_computation.12 | async-start | bytes 5013504 | tf_op jit(solution)/shard_map/reduce_scatter | solution.py:110
  192.5 9.3 %slice-start.6 = ((s8[5308416]{0:T(1024)(128)(4,1)}), s8[4194304]{0:T(1024)(128)(4,1)S(1)}, s32[]{:S(2)}) async-start(s8[5308416]{0:T(1024)(128)(4,1)} %bitcast.199), calls=%async_computation.19 | async-start | bytes 8388608
  192.5 12.8 %slice-start.2 = ((s8[5308416]{0:T(1024)(128)(4,1)}), s8[4194304]{0:T(1024)(128)(4,1)S(1)}, s32[]{:S(2)}) async-start(s8[5308416]{0:T(1024)(128)(4,1)} %bitcast.195), calls=%async_computation.15 | async-start | bytes 8388608
  195.4 6.3 %slice-start.7 = ((s8[5308416]{0:T(1024)(128)(4,1)}), s8[1114112]{0:T(1024)(128)(4,1)S(1)}, s32[]{:S(2)}) async-start(s8[5308416]{0:T(1024)(128)(4,1)} %bitcast.199), calls=%async_computation.20 | async-start | bytes 2228224
  195.4 9.9 %slice-start.3 = ((s8[5308416]{0:T(1024)(128)(4,1)}), s8[1114112]{0:T(1024)(128)(4,1)S(1)}, s32[]{:S(2)}) async-start(s8[5308416]{0:T(1024)(128)(4,1)} %bitcast.195), calls=%async_computation.16 | async-start | bytes 2228224
  208.9 3.7 copy-start.6
  222.7 84.9 %all-to-all-start.4 = ((bf16[16,2,2304]{2,1,0:T(2,128)(2,1)}), bf16[16,2,2304]{2,1,0:T(2,128)(2,1)S(1)}, u32[]{:S(2)}, u32[]{:S(2)}) async-start(bf16[16,2,2304]{2,1,0:T(2,128)(2,1)} %reshape.627), calls=%async_computation.4 | async-start | bytes 294912 | tf_op jit(solution)/shard_map/all_to_all | solution.py:116
  307.7 108.8 %all-to-all-start.5 = ((bf16[16,2,2304]{2,1,0:T(2,128)(2,1)}), bf16[16,2,2304]{2,1,0:T(2,128)(2,1)S(1)}, u32[]{:S(2)}, u32[]{:S(2)}) async-start(bf16[16,2,2304]{2,1,0:T(2,128)(2,1)} %reshape.629), calls=%async_computation.6 | async-start | bytes 294912 | tf_op jit(solution)/shard_map/all_to_all | solution.py:117
  408.2 24.0 %copy-start.1 = (s32[16,2]{0,1:T(2,128)S(1)}, s32[16,2]{0,1:T(2,128)}, u32[]{:S(2)}) copy-start(s32[16,2]{0,1:T(2,128)} %param.22) | copy-start | bytes 388
  416.5 13.1 %all-to-all-start.6 = ((bf16[16,2,2304]{2,1,0:T(2,128)(2,1)}), bf16[16,2,2304]{2,1,0:T(2,128)(2,1)S(1)}, u32[]{:S(2)}, u32[]{:S(2)}) async-start(bf16[16,2,2304]{2,1,0:T(2,128)(2,1)} %reshape.631), calls=%async_computation.8 | async-start | bytes 294912 | tf_op jit(solution)/shard_map/all_to_all | solution.py:118
Sparse Core Ops, SparseCore 0:
  31.9 59.9 all-gather.2
  94.7 65.9 all-gather.4
  192.6 105.8 reduce-scatter.2
  303.2 103.9 reduce-scatter.4
where the time goes:
time: 448 us; the launch traced here: 439 us
  waiting for transfers between devices  227 us (51%)
  matrix products  52.5 us (12%)
  other arithmetic  41.3 us (9%)
  local copies, waits for them, and re-layouts  39.8 us (9%)
  starting transfers between devices  31.7 us (7%)
  blocking collectives  28.5 us (6%)
  between operations  18.1 us (4%)
    reduce_scatter x1, waiting for transfers between devices, local(): lax.psum_scatter(results[2], 'frame', scatter_dimension=0, tiled=True)  95 us
    reduce_scatter x1, waiting for transfers between devices, local(): lax.psum_scatter(results[1], 'frame', scatter_dimension=0, tiled=True)  70.9 us
    all_gather x1, waiting for transfers between devices, local(): lax.all_gather(v_wide, 'frame', axis=0, tiled=True)  45.3 us
    unnamed x11, other arithmetic  29.2 us
    all_to_all x1, blocking collectives, local(): lax.all_to_all(keys_in, 'within', split_axis=2, concat_axis=1, tiled=True)  17.1 us
    unnamed x57, local copies, waits for them, and re-layouts  16.9 us
    all_to_all x1, starting transfers between devices, local(): lax.all_to_all(queries, 'within', split_axis=2, concat_axis=1, tiled=True)  14.1 us
    dot_general x3, matrix products, grads(): jnp.einsum('hqk,qhd->khd', prob_low, cotan3, preferred_element_type=jnp.f...  13.4 us
  transfers between devices with their start and end apart: 9, of which 6 were waited for; matrix products, arithmetic and copies ran while one was open for 19% of the time, Pallas kernels for 0%

commit v1 on v0

--- a/solution.py
+++ b/solution.py
@@ -1,9 +1,25 @@
+import functools
 import jax
 import jax.numpy as jnp
 from jax import lax
 from jax.sharding import PartitionSpec as P
 
 DH = 64
+
+
+def frames_return_all(z, array_axis, out_dim):
+    return jnp.concatenate(
+        lax.all_to_all(
+            jnp.stack(jnp.split(z, lax.axis_size("within"), axis=array_axis), axis=0),
+            "within",
+            0,
+            0,
+        ),
+        axis=out_dim,
+    )
+
+
+meet_samples = functools.partial(frames_return_all, array_axis=1, out_dim=2)
 
 
 def local(queries, keys_in, values_in, grad_out, partners, registers):
@@ -115,7 +131,7 @@
     return (
         lax.all_to_all(dq_low, "within", split_axis=1, concat_axis=2, tiled=True),
         lax.all_to_all(dk_low, "within", split_axis=1, concat_axis=2, tiled=True),
-        lax.all_to_all(dv_low, "within", split_axis=1, concat_axis=2, tiled=True),
+        meet_samples(dv_low),
     )
 
 

time: 448 us -> 453 us (1.011)
  local copies, waits for them, and re-layouts: 39.8 us -> 47.2 us
    reduce_scatter x1, waiting for transfers between devices: 95 us -> 64.9 us  [local(): lax.psum_scatter(results[2], 'frame', scatter_dimension=0, tiled=True)]
    reduce_scatter x1, waiting for transfers between devices: 70.9 us -> 99.2 us  [local(): lax.psum_scatter(results[1], 'frame', scatter_dimension=0, tiled=True)]
    unnamed x57 -> x63, local copies, waits for them, and re-layouts: 16.9 us -> 26.5 us
    all_to_all x1, waiting for transfers between devices: 0.01 us -> 7.11 us  [local(): lax.all_to_all(dk_low, 'within', split_axis=1, concat_axis=2, tiled=True)]
    unnamed x11 -> x8, other arithmetic: 29.2 us -> 23.4 us
  transfers between devices with their start and end apart: 9 -> 9, of which waited for: 6 -> 7; matrix products, arithmetic and copies ran while one was open for 19% -> 22% of each run, Pallas kernels for 0% -> 0%
where the time goes in v1:
time: 453 us; the launch traced here: 444 us
  waiting for transfers between devices  231 us (51%)
  matrix products  48.1 us (11%)
  local copies, waits for them, and re-layouts  47.2 us (10%)
  other arithmetic  40.1 us (9%)
  starting transfers between devices  31.6 us (7%)
  blocking collectives  28.5 us (6%)
  between operations  18.3 us (4%)
    reduce_scatter x1, waiting for transfers between devices, local(): lax.psum_scatter(results[1], 'frame', scatter_dimension=0, tiled=True)  99.2 us
    reduce_scatter x1, waiting for transfers between devices, local(): lax.psum_scatter(results[2], 'frame', scatter_dimension=0, tiled=True)  64.9 us
    all_gather x1, waiting for transfers between devices, local(): lax.all_gather(v_wide, 'frame', axis=0, tiled=True)  44.4 us
    unnamed x63, local copies, waits for them, and re-layouts  26.5 us
    unnamed x8, other arithmetic  23.4 us
    all_to_all x1, blocking collectives, local(): lax.all_to_all(keys_in, 'within', split_axis=2, concat_axis=1, tiled=True)  17.1 us
    all_to_all x1, starting transfers between devices, local(): lax.all_to_all(queries, 'within', split_axis=2, concat_axis=1, tiled=True)  15.2 us
    convert_element_type x1, other arithmetic, grads(): dscore_low = dscore.astype(jnp.bfloat16)  12.5 us
  transfers between devices with their start and end apart: 9, of which 7 were waited for; matrix products, arithmetic and copies ran while one was open for 22% of the time, Pallas kernels for 0%

profile of v1, /device:TPU:2, one launch (start us, length us, event | category | flops | bytes accessed | tf_op | source)
XLA Modules:
  0.0 444.4 jit_solution(3157966395684400098)
XLA Ops:
  7.2 1.3 copy.61
  9.1 2.4 reduce.55
  12.1 17.1 %all_to_all.107 = bf16[16,2,2304]{2,1,0:T(2,128)(2,1)S(1)} all-to-all(bf16[16,2,2304]{2,1,0:T(2,128)(2,1)S(1)} %reshape.633), channel_id=1, replica_groups=mesh['frame'=16,'within'=16] {'within'}, dimensions={0} | all-to-all | bytes 294912 | tf_op jit(solution)/shard_map/all_to_all | solution.py:28
  31.1 0.9 all_to_all.83
  32.1 1.2 copy.70
  33.4 2.4 reduce.57
  36.3 11.4 %all_to_all.108 = bf16[16,2,2304]{2,1,0:T(2,128)(2,1)S(1)} all-to-all(bf16[16,2,2304]{2,1,0:T(2,128)(2,1)S(1)} %reshape.629), channel_id=1, replica_groups=mesh['frame'=16,'within'=16] {'within'}, dimensions={0} | all-to-all | bytes 294912 | tf_op jit(solution)/shard_map/all_to_all | solution.py:29
  47.7 0.9 reshape.630
  49.6 0.9 all_to_all.90
  51.0 2.4 reduce.54
  53.4 1.2 reshape.631
  54.6 15.2 %all-to-all-start = ((bf16[16,2,2304]{2,1,0:T(2,128)(2,1)}), bf16[16,2,2304]{2,1,0:T(2,128)(2,1)S(1)}, u32[]{:S(2)}, u32[]{:S(2)}) async-start(bf16[16,2,2304]{2,1,0:T(2,128)(2,1)} %reshape.631), calls=%async_computation | async-start | bytes 294912 | tf_op jit(solution)/shard_map/all_to_all | solution.py:27
  73.3 2.4 reduce.56
  75.7 1.2 reshape.627
  78.8 8.2 %all-to-all-done = bf16[16,2,2304]{2,1,0:T(2,128)(2,1)S(1)} async-done(((bf16[16,2,2304]{2,1,0:T(2,128)(2,1)}), bf16[16,2,2304]{2,1,0:T(2,128)(2,1)S(1)}, u32[]{:S(2)}, u32[]{:S(2)}) %all-to-all-start) | async-done | bytes 147488 | tf_op jit(solution)/shard_map/all_to_all | solution.py:27
  87.0 3.5 all-to-all-start.2
  93.3 0.9 reshape.632
  95.4 3.4 all-to-all-done.2
  101.0 0.9 fusion.89
  102.0 2.3 copy-done.2
  104.2 3.7 fusion.2
  107.9 4.2 fusion.88
  112.1 4.2 fusion.87
  116.4 44.4 %all-gather.5.cloned.1.call-done = bf16[16,1152,64]{1,2,0:T(8,128)(2,1)} async-done(((bf16[1,1152,64]{1,2,0:T(8,128)(2,1)}), bf16[16,1152,64]{1,2,0:T(8,128)(2,1)}) %all-gather.5.cloned.1.call-update) | async-done | bytes 2359312 | tf_op jit(solution)/shard_map/all_gather | solution.py:101
  160.7 6.6 %fusion.3 = (f32[1152]{0:T(1024)S(1)}, f32[1152]{0:T(1024)S(1)}, f32[1152,1152]{0,1:T(8,128)}) fusion(f32[1152,1152]{0,1:T(8,128)} %get-tuple-element.110, f32[1152]{0:T(1024)S(1)} %get-tuple-element.109, bf16[1152,64]{0,1:T(8,128)(2,1)S(1)} %reshape.613, bf16[16,1152,64]{1,2,0:T(8,128)(2,1)} %all-gather.5.cloned.1.call-done, s32[]{:T(128)} %select_n.48), kind=kOutput, calls=%fused_computation.18 | convolution fusion | flops 175175424 | bytes 10926080 | tf_op jit(solution)/shard_map/qhd,khd->hqk/dot_general | solution.py:65
  167.3 5.1 %fusion.4 = (f32[1152]{0:T(1024)S(1)}, f32[1152]{0:T(1024)S(1)}, f32[1152,1152]{0,1:T(8,128)}) fusion(f32[1152,1152]{0,1:T(8,128)S(1)} %copy-done.3, f32[1152]{0:T(1024)S(1)} %get-tuple-element.106, bf16[1152,64]{0,1:T(8,128)(2,1)S(1)} %reshape.613, bf16[16,1152,64]{1,2,0:T(8,128)(2,1)} %all-gather.5.cloned.1.call-done, s32[]{:T(128)} %select_n.50), kind=kOutput, calls=%fused_computation.19 | convolution fusion | flops 175175424 | bytes 10926080 | tf_op jit(solution)/shard_map/qhd,khd->hqk/dot_general | solution.py:65
  172.4 2.9 broadcast_in_dim.64.clone.1
  175.3 2.6 fusion.20
  177.9 3.6 fusion.32
  181.6 3.6 fusion.44
  185.2 12.5 %multiply_convert_fusion.1 = (bf16[1152,1152]{0,1:T(8,128)(2,1)S(1)}, bf16[1152,1152]{0,1:T(8,128)(2,1)S(1)}, bf16[1152,1152]{0,1:T(8,128)(2,1)S(1)}) fusion(f32[1152,1152]{0,1:T(8,128)} %get-tuple-element.113, f32[1152]{0:T(1024)S(1)} %get-tuple-element.96, f32[1152]{0:T(1024)S(1)} %get-tuple-element.95, f32[1152,1152]{0,1:T(8,128)} %get-tuple-element.110, ...), kind=kLoop, calls=%fused_computation.6 | loop fusion | flops 19906560 | bytes 39826944 | tf_op jit(solution)/shard_map/convert_element_type | solution.py:83
  197.8 2.9 broadcast_in_dim.64.clone
  200.7 2.3 fusion.48
  203.0 3.0 fusion.53
  206.0 2.9 fusion.57
  209.0 2.9 convolution_multiply_fusion.7
  212.5 1.9 fusion.59
  215.1 6.8 %reduce.58 = bf16[1152,64]{1,0:T(8,128)(2,1)S(1)} reduce(bf16[1152,1,64]{2,1,0:T(2,128)(2,1)S(1)} %bitcast.258, bf16[]{:T(256)} %broadcast.338), dimensions={1}, to_apply=%bitcast.220.reduce_sub_computation | reduce | bytes 294914
  222.7 4.4 all-to-all-start.4
  227.2 64.9 %reduce-scatter.5.cloned.1.call-done = f32[1,1152,64]{1,2,0:T(8,128)} async-done(((f32[16,1152,64]{1,2,0:T(8,128)}), f32[1,1152,64]{1,2,0:T(8,128)}) %reduce-scatter.5.cloned.1.call-update) | async-done | bytes 294928 | tf_op jit(solution)/shard_map/reduce_scatter | solution.py:126
  292.0 1.0 convert_element_type.71
  301.7 99.2 %reduce-scatter.3.cloned.1.call-done = f32[1,1152,64]{1,2,0:T(8,128)} async-done(((f32[16,1152,64]{1,2,0:T(8,128)}), f32[1,1152,64]{1,2,0:T(8,128)}) %reduce-scatter.3.cloned.1.call-update) | async-done | bytes 294928 | tf_op jit(solution)/shard_map/reduce_scatter | solution.py:125
  400.9 1.0 convert_element_type.67
  402.6 6.8 %reduce.59 = bf16[1152,64]{1,0:T(8,128)(2,1)S(1)} reduce(bf16[1152,1,64]{2,1,0:T(2,128)(2,1)S(1)} %bitcast.257, bf16[]{:T(256)} %broadcast.338), dimensions={1}, to_apply=%bitcast.222.reduce_sub_computation | reduce | bytes 294914
  411.0 4.6 %all-to-all-start.5 = ((bf16[16,2,2304]{2,1,0:T(2,128)(2,1)}), bf16[16,2,2304]{2,1,0:T(2,128)(2,1)S(1)}, u32[]{:S(2)}, u32[]{:S(2)}) async-start(bf16[16,2,2304]{2,1,0:T(2,128)(2,1)} %reshape.637), calls=%async_computation.6 | async-start | bytes 294912 | tf_op jit(solution)/shard_map/all_to_all | solution.py:133
  416.9 7.1 %all-to-all-done.5 = bf16[16,2,2304]{2,1,0:T(2,128)(2,1)S(1)} async-done(((bf16[16,2,2304]{2,1,0:T(2,128)(2,1)}), bf16[16,2,2304]{2,1,0:T(2,128)(2,1)S(1)}, u32[]{:S(2)}, u32[]{:S(2)}) %all-to-all-start.5) | async-done | bytes 147488 | tf_op jit(solution)/shard_map/all_to_all | solution.py:133
  424.0 3.8 all-to-all-start.6
  433.2 3.5 all-to-all-done.6
  (103 shorter events, 33.5 us)
Async XLA Ops:
  7.2 62.6 %copy-start = (s32[16,2]{0,1:T(2,128)S(1)}, s32[16,2]{0,1:T(2,128)}, u32[]{:S(2)}) copy-start(s32[16,2]{0,1:T(2,128)} %param.22) | copy-start | bytes 388
  7.2 43.4 %copy-start.7 = (bf16[1,72,1024]{2,1,0:T(8,128)(2,1)S(1)}, bf16[1,72,1024]{2,1,0:T(8,128)(2,1)}, u32[]{:S(2)}) copy-start(bf16[1,72,1024]{2,1,0:T(8,128)(2,1)} %param.18) | copy-start | bytes 442372
  7.2 100.7 %all-gather.3.cloned.1.call-start = ((), (), s32[]{:S(2)}) async-start(), calls=%async_computation.9 | async-start | bytes 2506752 | tf_op jit(solution)/shard_map/all_gather | solution.py:100
  12.1 60.8 %copy-start.8 = (bf16[1,72,1024]{2,1,0:T(8,128)(2,1)S(1)}, bf16[1,72,1024]{2,1,0:T(8,128)(2,1)}, u32[]{:S(2)}) copy-start(bf16[1,72,1024]{2,1,0:T(8,128)(2,1)} %param.21) | copy-start | bytes 442372
  30.4 47.7 %copy-start.9 = (s32[16]{0:T(128)S(1)}, s32[16]{0:T(128)}, u32[]{:S(2)}) copy-start(s32[16]{0:T(128)} %param.23) | copy-start | bytes 196
  30.7 61.2 %copy-start.10 = (s32[3]{0:T(128)S(1)}, s32[3]{0:T(128)}, u32[]{:S(2)}) copy-start(s32[3]{0:T(128)} %constant.142.clone.1) | copy-start | bytes 40
  32.0 128.7 %all-gather.5.cloned.1.call-start = ((), (), s32[]{:S(2)}) async-start(), calls=%async_computation.10 | async-start | bytes 2506752 | tf_op jit(solution)/shard_map/all_gather | solution.py:101
  54.6 32.4 %all-to-all-start = ((bf16[16,2,2304]{2,1,0:T(2,128)(2,1)}), bf16[16,2,2304]{2,1,0:T(2,128)(2,1)S(1)}, u32[]{:S(2)}, u32[]{:S(2)}) async-start(bf16[16,2,2304]{2,1,0:T(2,128)(2,1)} %reshape.631), calls=%async_computation | async-start | bytes 294912 | tf_op jit(solution)/shard_map/all_to_all | solution.py:27
  87.0 11.9 %all-to-all-start.2 = ((bf16[16,2,2304]{2,1,0:T(2,128)(2,1)}), bf16[16,2,2304]{2,1,0:T(2,128)(2,1)S(1)}, u32[]{:S(2)}, u32[]{:S(2)}) async-start(bf16[16,2,2304]{2,1,0:T(2,128)(2,1)} %reshape.627), calls=%async_computation.2 | async-start | bytes 294912 | tf_op jit(solution)/shard_map/all_to_all | solution.py:30
  90.5 201.6 %reduce-scatter.5.cloned.1.call-start = ((), (), s32[]{:S(2)}) async-start(), calls=%async_computation.12 | async-start | bytes 5013504 | tf_op jit(solution)/shard_map/reduce_scatter | solution.py:126
  102.0 2.3 copy-start.2
  160.7 6.6 %copy-start.3 = (f32[1152,1152]{0,1:T(8,128)S(1)}, f32[1152,1152]{0,1:T(8,128)}, u32[]{:S(2)}) copy-start(f32[1152,1152]{0,1:T(8,128)} %get-tuple-element.107) | copy-start | bytes 15925252
  160.7 14.6 %slice-start = ((s8[5308416]{0:T(1024)(128)(4,1)}), s8[4194304]{0:T(1024)(128)(4,1)S(1)}, s32[]{:S(2)}) async-start(s8[5308416]{0:T(1024)(128)(4,1)} %bitcast.253), calls=%async_computation.13 | async-start | bytes 8388608
  167.3 8.0 %slice-start.1 = ((s8[5308416]{0:T(1024)(128)(4,1)}), s8[1114112]{0:T(1024)(128)(4,1)S(1)}, s32[]{:S(2)}) async-start(s8[5308416]{0:T(1024)(128)(4,1)} %bitcast.253), calls=%async_computation.14 | async-start | bytes 2228224
  172.4 5.5 %slice-start.2 = ((s8[5308416]{0:T(1024)(128)(4,1)}), s8[4194304]{0:T(1024)(128)(4,1)S(1)}, s32[]{:S(2)}) async-start(s8[5308416]{0:T(1024)(128)(4,1)} %bitcast.255), calls=%async_computation.15 | async-start | bytes 8388608
  175.3 2.6 slice-start.3
  185.2 215.8 %reduce-scatter.3.cloned.1.call-start = ((), (), s32[]{:S(2)}) async-start(), calls=%async_computation.11 | async-start | bytes 5013504 | tf_op jit(solution)/shard_map/reduce_scatter | solution.py:125
  197.7 8.3 %copy-start.5 = (bf16[1152,1152]{0,1:T(8,128)(2,1)}, bf16[1152,1152]{0,1:T(8,128)(2,1)S(1)}, u32[]{:S(2)}) copy-start(bf16[1152,1152]{0,1:T(8,128)(2,1)S(1)} %get-tuple-element.97) | copy-start | bytes 7962628
  197.8 8.3 %copy-start.4 = (bf16[1152,1152]{0,1:T(8,128)(2,1)}, bf16[1152,1152]{0,1:T(8,128)(2,1)S(1)}, u32[]{:S(2)}) copy-start(bf16[1152,1152]{0,1:T(8,128)(2,1)S(1)} %get-tuple-element.98) | copy-start | bytes 7962628
  209.0 3.5 copy-start.6
  222.7 188.2 %all-to-all-start.4 = ((bf16[16,2,2304]{2,1,0:T(2,128)(2,1)}), bf16[16,2,2304]{2,1,0:T(2,128)(2,1)S(1)}, u32[]{:S(2)}, u32[]{:S(2)}) async-start(bf16[16,2,2304]{2,1,0:T(2,128)(2,1)} %reshape.635), calls=%async_computation.4 | async-start | bytes 294912 | tf_op jit(solution)/shard_map/all_to_all | solution.py:132
  227.1 210.3 %copy-start.1 = (s32[16,2]{0,1:T(2,128)S(1)}, s32[16,2]{0,1:T(2,128)}, u32[]{:S(2)}) copy-start(s32[16,2]{0,1:T(2,128)} %param.22) | copy-start | bytes 388
  411.0 13.1 %all-to-all-start.5 = ((bf16[16,2,2304]{2,1,0:T(2,128)(2,1)}), bf16[16,2,2304]{2,1,0:T(2,128)(2,1)S(1)}, u32[]{:S(2)}, u32[]{:S(2)}) async-start(bf16[16,2,2304]{2,1,0:T(2,128)(2,1)} %reshape.637), calls=%async_computation.6 | async-start | bytes 294912 | tf_op jit(solution)/shard_map/all_to_all | solution.py:133
  424.0 12.6 %all-to-all-start.6 = ((bf16[16,1,72,64]{2,3,1,0:T(8,128)(2,1)}), bf16[16,1,72,64]{2,3,1,0:T(8,128)(2,1)S(1)}, u32[]{:S(2)}, u32[]{:S(2)}) async-start(bf16[16,1,72,64]{2,3,1,0:T(8,128)(2,1)} %constant_dynamic-update-slice_fusion), calls=%async_computation.8 | async-start | bytes 524288 | tf_op jit(solution)/shard_map/all_to_all | solution.py:12
Sparse Core Ops, SparseCore 0:
  32.2 61.7 all-gather.2
  96.7 63.9 all-gather.4
  185.3 106.7 reduce-scatter.4
  296.9 104.0 reduce-scatter.2
